TPU v7x, 32 devices: a whole 2x2x4 slice. The times are simulated.
32 devices in a mesh: blk: 32 (over z, y, x, core).
Axes of the slice: x: 2, y: 2, z: 4, core: 2. Of those that a mesh axis runs over, the one named last changes fastest.
Arguments:
- hidden: bfloat16 [64, 2048], P('blk')
- norm_gain: float32 [2048], replicated, may hold values from 0.5 to 1.5
- head_weight: bfloat16 [102400, 2048], P('blk')
- targets: int32 [64], P('blk'), may hold values from 0 to 102399
- spans: int32 [32, 2], P('blk'), may hold values from 0 to 2, as said below
Outputs:
- logprob: float32 [64], P('blk')
- entropy: float32 [64], P('blk')
Inputs may be any that keep to these rules, and one draw needn't show every extreme that they name: 0 <= spans[k, 0] < spans[k, 1] <= 2; some device has the whole piece scored.
All inputs are finite; a program needn't handle non-finite values.
Results may differ from a plain program's by a relative error of at most 0.00073.
Values may be sent and summed in bfloat16 or wider, within the bound.
A program may use at most 64 MiB of HBM per device.

v0:
```python
import jax
import jax.numpy as jnp
from jax import lax
from jax.sharding import PartitionSpec as P

epsilon = 1e-06


def merged_2(value, axis, join):
    pieces = jax.tree.map(lambda part: lax.all_gather(part, axis), value)
    head = jax.tree.map(lambda part: part[0], pieces)
    tail = jax.tree.map(lambda part: part[1:], pieces)
    total, _ = lax.scan(lambda total, piece: (join(total, piece), None), head, tail)
    return total


def combine(first, second):
    peak = jnp.maximum(first[0], second[0])
    scale_one = jnp.exp(first[0] - peak)
    scale_two = jnp.exp(second[0] - peak)
    return (
        peak,
        first[1] * scale_one + second[1] * scale_two,
        first[2] * scale_one + second[2] * scale_two,
        first[3] + second[3],
    )


def logits_of(head_weight, piece_rows):
    return lax.dot_general(
        head_weight, piece_rows, (((1,), (1,)), ((), ())), preferred_element_type=jnp.float32
    )


def target_logit(logits, piece_targets, col_first):
    col_ids = col_first + jnp.arange(logits.shape[0], dtype=jnp.int32)
    return jnp.sum(
        jnp.where(col_ids[:, None] == piece_targets[None, :], logits, jnp.float32(0.0)), axis=0
    )


def block_stats(piece_rows, piece_targets, head_weight, col_first):
    logits = logits_of(head_weight, piece_rows)
    peak = jnp.max(logits, axis=0)
    expon = jnp.exp(logits - peak[None, :])
    return (
        peak,
        jnp.sum(expon, axis=0),
        jnp.sum(expon * logits, axis=0),
        target_logit(logits, piece_targets, col_first),
    )


def stats_of(piece_rows, piece_targets, head_weight, col_first):
    row_count = piece_rows.shape[0]
    block_rows = max(
        (size_try for size_try in range(1, min(row_count, 512) + 1) if row_count % size_try == 0)
    )
    if block_rows == row_count:
        return block_stats(piece_rows, piece_targets, head_weight, col_first)
    grouped_rows = piece_rows.reshape(row_count // block_rows, block_rows, piece_rows.shape[1])
    grouped_targets = piece_targets.reshape(row_count // block_rows, block_rows)
    results = lax.map(
        lambda pair: block_stats(pair[0], pair[1], head_weight, col_first),
        (grouped_rows, grouped_targets),
    )
    return tuple((item.reshape(row_count) for item in results))


def finish(lse, expsum, moment, picked, scored):
    logprob = jnp.where(scored, picked - lse, jnp.float32(0.0))
    entropy = jnp.where(scored, lse - moment / expsum, jnp.float32(0.0))
    return (logprob, entropy)


def local(hidden, norm_gain, head_weight, targets, spans):
    own_rows = hidden.shape[0]
    vocab_local = head_weight.shape[0]
    position = lax.axis_index("blk")
    col_first = position * vocab_local
    values = hidden.astype(jnp.float32)
    meansq = jnp.mean(values * values, axis=-1, keepdims=True)
    normed = (values * lax.rsqrt(meansq + epsilon) * norm_gain).astype(jnp.bfloat16)
    slot_ids = jnp.arange(own_rows, dtype=jnp.int32)
    scored = (slot_ids >= spans[0, 0]) & (slot_ids < spans[0, 1])
    fresh = stats_of(
        lax.all_gather(normed, "blk", axis=0, tiled=True),
        lax.all_gather(targets, "blk", axis=0, tiled=True),
        head_weight,
        col_first,
    )
    partial_stats = tuple((fresh[index_stat] for index_stat in range(4)))
    merged = merged_2(partial_stats, "blk", combine)
    own = tuple(
        (lax.dynamic_slice_in_dim(item, position * own_rows, own_rows, 0) for item in merged)
    )
    lse = own[0] + jnp.log(own[1])
    return finish(lse, own[1], own[2], own[3], scored)


def solution(mesh):
    return jax.shard_map(
        local,
        mesh=mesh,
        in_specs=(P("blk", None), P(), P("blk", None), P("blk"), P("blk", None)),
        out_specs=(P("blk"), P("blk")),
        check_vma=False,
    )
```

profile of v0, /device:TPU:0, one launch (start us, length us, event | category | flops | bytes accessed | tf_op | source)
XLA Modules:
  0.0 141.0 jit_solution(1277375752029213388)
XLA Ops:
  0.6 0.0 copy-start.1
  0.6 0.0 copy-start
  0.6 0.8 fusion.14
  1.5 0.8 fusion.17
  2.3 43.9 %all-gather.4 = bf16[32,2,2048]{2,1,0:T(2,128)(2,1)S(1)} all-gather(bf16[1,2,2048]{2,1,0:T(2,128)(2,1)S(1)} %fusion.17), channel_id=1, replica_groups=mesh['blk'=32] {'blk'}, dimensions={0}, use_global_device_ids=true | all-gather | bytes 270336 | tf_op jit(solution)/shard_map/all_gather | solution.py:87
  46.2 0.1 reshape.46
  46.3 8.9 %fusion.20 = (f32[64]{0:T(128)S(1)}, f32[64,3200]{1,0:T(8,128)S(1)}) fusion(bf16[64,2048]{1,0:T(8,128)(2,1)S(1)} %reshape.46, bf16[3200,2048]{1,0:T(8,128)(2,1)} %param.9), kind=kOutput, calls=%fused_computation.36 | convolution fusion | flops 839065536 | bytes 14188800 | tf_op jit(solution)/shard_map/dot_general | solution.py:30
  55.3 0.0 copy-done.1
  55.3 0.2 dynamic-update-slice.3
  55.5 36.9 %all-reduce.3 = s32[64]{0:T(128)S(1)} all-reduce(s32[64]{0:T(128)S(1)} %dynamic-update-slice.3), channel_id=1, replica_groups=mesh['blk'=32] {'blk'}, use_global_device_ids=true, to_apply=%add.3 | all-reduce | flops 64 | bytes 512
  92.4 0.4 fusion.12
  92.8 0.3 dynamic-update-slice.2
  93.1 0.3 dynamic-update-slice.4
  93.3 0.3 dynamic-update-slice.1
  93.6 0.3 dynamic-update-slice
  93.8 41.6 %all-reduce.5 = (f32[2048]{0:T(1024)S(1)}, f32[2048]{0:T(1024)S(1)}, f32[2048]{0:T(1024)S(1)}, f32[2048]{0:T(1024)S(1)}) all-reduce(f32[2048]{0:T(1024)S(1)} %dynamic-update-slice, f32[2048]{0:T(1024)S(1)} %dynamic-update-slice.1, f32[2048]{0:T(1024)S(1)} %dynamic-update-slice.2, ...), channel_id=2, replica_groups=mesh['blk'=32] {'blk'}, use_global_device_ids=true, to_apply=%add | all-reduce | flops 8192 | bytes 65536
  135.4 0.1 slice.52
  135.5 0.1 reshape.31
  135.6 0.1 slice.53
  135.6 0.1 reshape.32
  135.7 0.1 slice.54
  135.8 0.1 reshape.33
  135.9 0.1 slice.55
  135.9 0.1 reshape.34
  136.0 2.5 %while.16 = (s32[]{:T(128)}, f32[64]{0:T(128)S(1)}, f32[64]{0:T(128)S(1)}, f32[64]{0:T(128)S(1)}, f32[64]{0:T(128)S(1)}, /*index=5*/f32[31,64]{1,0:T(8,128)S(1)}...) while((s32[]{:T(128)}, f32[64]{0:T(128)S(1)}, f32[64]{0:T(128)S(1)}, ...), condition=%wide.region_6.7_spmd, body=%wide.region_5.6_spmd.sunk | while | flops 770 | bytes 4461 | solution.py:13
  138.5 0.0 copy-done
  138.6 0.6 fusion.19
  139.2 1.8 %subtract_select_fusion = (f32[2]{0:T(128)}, f32[2]{0:T(128)}) fusion(f32[64]{0:T(128)S(1)} %get-tuple-element.55, s32[]{:T(128)S(6)} %select_n.18, s32[]{:T(128)} %bitcast.5, s32[]{:T(128)} %bitcast.4, f32[64]{0:T(128)S(1)} %get-tuple-element.54, f32[64]{0:T(128)S(1)} %get-tuple-element.53, f32[64]{0:T(128)S(1)} %get-tuple-element.52), kind=kLoop, calls=%fused_computation.31 | loop fusion | flops 18 | bytes 60 | tf_op jit(solution)/shard_map/jit(_where)/select_n | solution.py:72
  (104 shorter events, 1.8 us)
Async XLA Ops:
  0.6 54.6 %copy-start.1 = (s32[2]{0:T(128)S(1)}, s32[2]{0:T(128)}, u32[]{:S(2)}) copy-start(s32[2]{0:T(128)} %param.10) | copy-start | bytes 28
  0.6 137.9 %copy-start = (s32[1,2]{1,0:T(1,128)S(1)}, s32[1,2]{1,0:T(1,128)}, u32[]{:S(2)}) copy-start(s32[1,2]{1,0:T(1,128)} %param.11) | copy-start | bytes 28
where the time goes:
time: 142 us; the launch traced here: 141 us
  blocking collectives  122 us (86%)
  matrix products  8.88 us (6%)
  other arithmetic  5.65 us (4%)
  local copies, waits for them, and re-layouts  2.64 us (2%)
    unnamed x2, blocking collectives  78.4 us
    all_gather x1, blocking collectives, local(): lax.all_gather(normed, 'blk', axis=0, tiled=True)  43.9 us
    dot_general x1, matrix products, logits_of(): lax.dot_general(head_weight, piece_rows, (((1,), (1,)), ((), ())), prefer...  8.88 us

commit v1 on v0

v1 whole, which is shorter than its diff:
```python
import functools

import jax
import jax.numpy as jnp
from jax import lax
from jax.experimental import pallas as pl
from jax.experimental.pallas import tpu as pltpu
from jax.sharding import PartitionSpec as P

epsilon = 1e-06
MESH = pl.DeviceIdType.MESH


def largest_block(count, limit, step):
    sizes = [size for size in range(step, min(count, limit) + 1, step) if count % size == 0]
    return max(sizes) if sizes else count


def split_of(n):
    cores = 2 if n % 2 == 0 else 1
    plane = 4 if n % (cores * 4) == 0 else 1
    return n // (cores * plane), plane, cores


def kernel(
    n, blocks, hidden_ref, gain_ref, weight_ref, targets_ref, spans_ref, logprob_ref, entropy_ref,
    hid, gain, weight, rows, wide, operand, logits, own_targets, all_targets, message,
    inbox, load_sem, weight_sem, row_send, row_recv, target_send, target_recv, stat_send, stat_recv,
):
    me = lax.axis_index("blk")
    slots, width = hid.shape
    chunks = width // 128
    piece = slots * chunks
    row_count = n * slots
    block = weight.shape[0] // blocks
    high_size, plane_size, core_size = split_of(n)

    loads = [
        pltpu.make_async_copy(hidden_ref, hid, load_sem.at[0]),
        pltpu.make_async_copy(gain_ref, gain, load_sem.at[1]),
    ]
    for load in loads:
        load.start()

    def weight_copy(index):
        where = pl.ds(index * block, block)
        return pltpu.make_async_copy(weight_ref.at[where], weight.at[where], weight_sem.at[index])

    for index in range(blocks):
        weight_copy(index).start()

    barrier = pltpu.get_barrier_semaphore()

    @pl.loop(1, n)
    def _(step):
        pl.semaphore_signal(barrier, inc=1, device_id=(lax.rem(me + step, n),), device_id_type=MESH)

    for load in loads:
        load.wait()

    values = hid[...].astype(jnp.float32)
    meansq = jnp.mean(values * values, axis=-1, keepdims=True)
    values = values * lax.rsqrt(meansq + epsilon)
    mine = wide.at[0]
    for chunk in range(chunks):
        mine[:, chunk, :] = values[:, chunk * 128 : (chunk + 1) * 128]
    start = pl.multiple_of(me * piece, piece)
    normed = (mine[...] * gain[...][None]).astype(jnp.bfloat16)
    rows[pl.ds(start, piece), :] = normed.reshape(piece, 128)

    lanes = lax.broadcasted_iota(jnp.int32, own_targets.shape, 1)
    spread = jnp.zeros(own_targets.shape, jnp.int32)
    for slot in range(slots):
        spread = jnp.where(lanes == slot * n + me, targets_ref[slot], spread)
    own_targets[...] = spread
    all_targets[me] = spread

    pl.semaphore_wait(barrier, n - 1)

    def index_of(high, plane, core):
        return (high * plane_size + plane) * core_size + core

    core = lax.rem(me, core_size)
    plane = lax.rem(me // core_size, plane_size)
    high = me // (core_size * plane_size)

    def row_copy(owner, device):
        where = pl.ds(pl.multiple_of(owner * piece, piece), piece)
        return pltpu.make_async_remote_copy(
            src_ref=rows.at[where],
            dst_ref=rows.at[where],
            send_sem=row_send,
            recv_sem=row_recv.at[owner],
            device_id=(device,),
            device_id_type=MESH,
        )

    def arrive(owner):
        row_copy(owner, me).wait_recv()

    def spread_plane(owner):
        for step in range(1, plane_size):
            row_copy(owner, index_of(high, lax.rem(plane + step, plane_size), core)).start()

    def spread_core(owner):
        for step in range(1, core_size):
            row_copy(owner, index_of(high, plane, lax.rem(core + step, core_size))).start()

    @pl.loop(1, high_size)
    def _(step):
        row_copy(me, index_of(lax.rem(high + step, high_size), plane, core)).start()

    spread_plane(me)
    spread_core(me)

    def target_copy(device):
        return pltpu.make_async_remote_copy(
            src_ref=own_targets,
            dst_ref=all_targets.at[me],
            send_sem=target_send,
            recv_sem=target_recv,
            device_id=(device,),
            device_id_type=MESH,
        )

    @pl.loop(1, high_size)
    def _(step):
        owner = index_of(lax.rem(high + step, high_size), plane, core)
        arrive(owner)
        spread_plane(owner)
        spread_core(owner)

    @pl.loop(0, high_size)
    def _(step):
        for other in range(1, plane_size):
            owner = index_of(
                lax.rem(high + step, high_size), lax.rem(plane + other, plane_size), core
            )
            arrive(owner)
            spread_core(owner)

    @pl.loop(1, n)
    def _(step):
        target_copy(lax.rem(me + step, n)).start()

    for other in range(1, core_size):

        @pl.loop(0, high_size)
        def _(step):
            for place in range(plane_size):
                arrive(index_of(step, place, lax.rem(core + other, core_size)))

    group = min(n, 32)

    @pl.loop(0, n // group)
    def _(index):
        first = pl.multiple_of(index * group * piece, group * piece)
        wide[...] = (
            rows[pl.ds(first, group * piece), :]
            .astype(jnp.float32)
            .reshape(group, slots, chunks, 128)
        )
        for slot in range(slots):
            place = pl.ds(pl.multiple_of(slot * n + index * group, group), group)
            for chunk in range(chunks):
                operand[place, chunk * 128 : (chunk + 1) * 128] = wide[:, slot, chunk, :].astype(
                    jnp.bfloat16
                )

    peak = None
    for index in range(blocks):
        weight_copy(index).wait()
        where = pl.ds(index * block, block)
        product = lax.dot_general(
            weight[where, :],
            operand[...],
            (((1,), (1,)), ((), ())),
            preferred_element_type=jnp.float32,
        )
        logits[where, :] = product
        top = jnp.max(product, axis=0, keepdims=True)
        peak = top if peak is None else jnp.maximum(peak, top)

    everyone = all_targets.at[pl.ds(0, n - 1)]
    pltpu.make_async_copy(everyone, everyone, target_recv).wait()
    wanted = jnp.sum(all_targets[...], axis=0)[:, :row_count] - me * weight.shape[0]
    found = logits[...]
    column = lax.broadcasted_iota(jnp.int32, found.shape, 0)
    expon = jnp.exp(found - peak)
    total = jnp.sum(expon, axis=0, keepdims=True)
    moment = jnp.sum(expon * found, axis=0, keepdims=True)
    picked = jnp.sum(jnp.where(column == wanted, found, 0.0), axis=0, keepdims=True)

    def by_slot(item):
        return [item[:, slot * n : (slot + 1) * n] for slot in range(slots)]

    blank = [jnp.zeros((1, n), jnp.float32)] * slots
    packed = jnp.concatenate(
        by_slot(total) + by_slot(moment) + by_slot(picked) + blank
        + by_slot(peak) + by_slot(peak) + blank + blank,
        axis=0,
    )
    turned = packed.T
    fields = turned.shape[1]
    turned = jnp.concatenate([turned, jnp.zeros((n, 128 - fields), jnp.float32)], axis=1)
    message[...] = turned.reshape(n, 1, 128)
    inbox[me] = message[me]

    def stat_copy(device):
        return pltpu.make_async_remote_copy(
            src_ref=message.at[device],
            dst_ref=inbox.at[me],
            send_sem=stat_send,
            recv_sem=stat_recv,
            device_id=(device,),
            device_id_type=MESH,
        )

    @pl.loop(1, n)
    def _(step):
        stat_copy(lax.rem(me + step, n)).start()

    others = inbox.at[pl.ds(0, n - 1)]
    pltpu.make_async_copy(others, others, stat_recv).wait()
    parts = inbox[...].reshape(n, 128)
    peaks = pltpu.roll(parts, 128 - fields // 2, 1)
    top = jnp.max(peaks, axis=0, keepdims=True)
    merged = jnp.sum(parts * jnp.exp(peaks - top), axis=0, keepdims=True)[:, :128]
    lse = top + jnp.log(merged)
    expected = pltpu.roll(merged, 128 - slots, 1) / merged
    chosen = pltpu.roll(merged, 128 - 2 * slots, 1)
    slot_ids = lax.broadcasted_iota(jnp.int32, (1, 128), 1)
    scored = (slot_ids >= spans_ref[0, 0]) & (slot_ids < spans_ref[0, 1])
    logprob_ref[...] = jnp.where(scored, chosen - lse, 0.0)[:, :slots]
    entropy_ref[...] = jnp.where(scored, lse - expected, 0.0)[:, :slots]

    sent = rows.at[pl.ds(0, (n - 1) * piece)]
    pltpu.make_async_copy(sent, sent, row_send).wait()
    pltpu.make_async_copy(everyone, everyone, target_send).wait()
    pltpu.make_async_copy(others, others, stat_send).wait()


def local(n, hidden, norm_gain, head_weight, targets, spans):
    slots, width = hidden.shape
    vocab = head_weight.shape[0]
    chunks = width // 128
    piece = slots * chunks
    row_count = n * slots
    blocks = vocab // largest_block(vocab, 1600, 16)
    lanes = max(128, row_count)
    group = min(n, 32)
    small = jax.ShapeDtypeStruct((1, slots), jnp.float32)
    logprob, entropy = pl.pallas_call(
        functools.partial(kernel, n, blocks),
        out_shape=(small, small),
        in_specs=[
            pl.BlockSpec(memory_space=pl.ANY),
            pl.BlockSpec(memory_space=pl.ANY),
            pl.BlockSpec(memory_space=pl.ANY),
            pl.BlockSpec(memory_space=pltpu.SMEM),
            pl.BlockSpec(memory_space=pltpu.SMEM),
        ],
        out_specs=(pl.BlockSpec(memory_space=pltpu.VMEM),) * 2,
        scratch_shapes=[
            pltpu.VMEM((slots, width), jnp.bfloat16),
            pltpu.VMEM((chunks, 128), jnp.float32),
            pltpu.VMEM((vocab, width), jnp.bfloat16),
            pltpu.VMEM((n * piece, 128), jnp.bfloat16),
            pltpu.VMEM((group, slots, chunks, 128), jnp.float32),
            pltpu.VMEM((row_count, width), jnp.bfloat16),
            pltpu.VMEM((vocab, row_count), jnp.float32),
            pltpu.VMEM((1, lanes), jnp.int32),
            pltpu.VMEM((n, 1, lanes), jnp.int32),
            pltpu.VMEM((n, 1, 128), jnp.float32),
            pltpu.VMEM((n, 1, 128), jnp.float32),
            pltpu.SemaphoreType.DMA((2,)),
            pltpu.SemaphoreType.DMA((blocks,)),
            pltpu.SemaphoreType.DMA,
            pltpu.SemaphoreType.DMA((n,)),
            pltpu.SemaphoreType.DMA,
            pltpu.SemaphoreType.DMA,
            pltpu.SemaphoreType.DMA,
            pltpu.SemaphoreType.DMA,
        ],
        compiler_params=pltpu.CompilerParams(
            collective_id=0, has_side_effects=True, vmem_limit_bytes=48 * 2**20
        ),
        name="head_stats",
    )(hidden, norm_gain.reshape(chunks, 128), head_weight, targets, spans)
    return logprob.reshape(slots), entropy.reshape(slots)


def solution(mesh):
    return jax.shard_map(
        functools.partial(local, mesh.shape["blk"]),
        mesh=mesh,
        in_specs=(P("blk", None), P(), P("blk", None), P("blk"), P("blk", None)),
        out_specs=(P("blk"), P("blk")),
        check_vma=False,
    )
```

time: 142 us -> 33.6 us (0.24)
  blocking collectives: 122 us -> 0 us
  Pallas kernels: 0 us -> 28.9 us
  matrix products: 8.88 us -> 0 us
  other arithmetic: 5.65 us -> 0 us
    unnamed x2 -> x0, blocking collectives: 78.4 us -> none
    all_gather x1 -> x0, blocking collectives: 43.9 us -> none  [local(): lax.all_gather(normed, 'blk', axis=0, tiled=True)]
    pallas_call x0 -> x1, Pallas kernels: none -> 28.9 us  [local(): pl.pallas_call(functools.partial(kernel, n, blocks), out_shape=(small, sm...]
    dot_general x1 -> x0, matrix products: 8.88 us -> none  [logits_of(): lax.dot_general(head_weight, piece_rows, (((1,), (1,)), ((), ())), prefer...]
    unnamed x15 -> x10, local copies, waits for them, and re-layouts: 1.41 us -> 3.72 us
    select_n x1 -> x0, other arithmetic: 1.85 us -> none  [finish(): entropy = jnp.where(scored, lse - moment / expsum, jnp.float32(0.0))]
    add x63 -> x0, other arithmetic: 1.75 us -> none  [the longest x31 0.93 us: combine(): first[1] * scale_one + second[1] * scale_two]
where the time goes in v1:
time: 33.6 us; the launch traced here: 33.3 us
  Pallas kernels  28.9 us (86%)
  local copies, waits for them, and re-layouts  3.72 us (11%)
  between operations  0.65 us (2%)
    pallas_call x1, Pallas kernels, local(): pl.pallas_call(functools.partial(kernel, n, blocks), out_shape=(small, sm...  28.9 us
    unnamed x10, local copies, waits for them, and re-layouts  3.72 us

profile of v1, /device:TPU:0, one launch (start us, length us, event | category | flops | bytes accessed | tf_op | source)
XLA Modules:
  0.0 33.3 jit_solution(12796957582800718413)
XLA Ops:
  0.6 0.0 copy-start
  0.6 0.7 %copy-done = bf16[2,2048]{1,0:T(2,128)(2,1)S(1)} copy-done((bf16[2,2048]{1,0:T(2,128)(2,1)S(1)}, bf16[2,2048]{1,0:T(2,128)(2,1)}, u32[]{:S(2)}) %copy-start) | copy-done | bytes 8216
  1.3 0.0 copy-start.1
  1.3 0.7 %copy-done.1 = f32[2048]{0:T(1024)S(1)} copy-done((f32[2048]{0:T(1024)S(1)}, f32[2048]{0:T(1024)}, u32[]{:S(2)}) %copy-start.1) | copy-done | bytes 8216
  2.0 0.0 copy-start.2
  2.0 0.7 %copy-done.2 = s32[2]{0:T(128)S(1)} copy-done((s32[2]{0:T(128)S(1)}, s32[2]{0:T(128)}, u32[]{:S(2)}) %copy-start.2) | copy-done | bytes 32
  2.7 0.0 copy-start.3
  2.7 0.7 %copy-done.3 = s32[1,2]{1,0:T(1,128)S(1)} copy-done((s32[1,2]{1,0:T(1,128)S(1)}, s32[1,2]{1,0:T(1,128)}, u32[]{:S(2)}) %copy-start.3) | copy-done | bytes 32
  3.3 28.9 %head_stats.1 = (f32[1,2]{1,0:T(1,128)S(1)}, f32[1,2]{1,0:T(1,128)S(1)}) custom-call(bf16[2,2048]{1,0:T(2,128)(2,1)S(1)} %copy-done, f32[16,128]{1,0:T(8,128)S(1)} %bitcast.3, bf16[3200,2048]{1,0:T(8,128)(2,1)} %weight_ref.1, s32[2]{0:T(128)S(1)} %copy-done.2, s32[1,2]{1,0:T(1,128)S(1)} %copy-done.3), custom_call_target="tpu_custom_call" | custom-call | tf_op jit(solution)/shard_map/head_stats/pallas_call | solution.py:253
  32.2 0.5 %copy.9 = f32[2]{0:T(128)} copy(f32[2]{0:T(128)S(1)} %bitcast.5) | data formatting | bytes 16
  32.8 0.5 %copy.10 = f32[2]{0:T(128)} copy(f32[2]{0:T(128)S(1)} %bitcast.4) | data formatting | bytes 16
Async XLA Ops:
  0.6 0.7 %copy-start = (bf16[2,2048]{1,0:T(2,128)(2,1)S(1)}, bf16[2,2048]{1,0:T(2,128)(2,1)}, u32[]{:S(2)}) copy-start(bf16[2,2048]{1,0:T(2,128)(2,1)} %hidden_ref.1) | copy-start | bytes 24580
  1.3 0.7 %copy-start.1 = (f32[2048]{0:T(1024)S(1)}, f32[2048]{0:T(1024)}, u32[]{:S(2)}) copy-start(f32[2048]{0:T(1024)} %param.6) | copy-start | bytes 24580
  2.0 0.7 %copy-start.2 = (s32[2]{0:T(128)S(1)}, s32[2]{0:T(128)}, u32[]{:S(2)}) copy-start(s32[2]{0:T(128)} %targets_ref.1) | copy-start | bytes 28
  2.7 0.7 %copy-start.3 = (s32[1,2]{1,0:T(1,128)S(1)}, s32[1,2]{1,0:T(1,128)}, u32[]{:S(2)}) copy-start(s32[1,2]{1,0:T(1,128)} %spans_ref.1) | copy-start | bytes 28

commit v2 on v1

v2 whole, which is shorter than its diff:
```python
import functools

import jax
import jax.numpy as jnp
from jax import lax
from jax.experimental import pallas as pl
from jax.experimental.pallas import tpu as pltpu
from jax.sharding import PartitionSpec as P

epsilon = 1e-06
MESH = pl.DeviceIdType.MESH


def largest_block(count, limit, step):
    sizes = [size for size in range(step, min(count, limit) + 1, step) if count % size == 0]
    return max(sizes) if sizes else count


def layout_of(n):
    size = 8 if n % 8 == 0 else n
    return size, n // size


def kernel(
    n, blocks, hidden_ref, gain_ref, weight_ref, targets_ref, spans_ref, out_ref,
    hid, gain, weight, small_targets, small_spans, rows, wide, operand, logits,
    all_targets, message, inbox, onward, last, load_sem, weight_sem,
    row_send, high_recv, near_recv, far_recv, target_send, target_high, target_near,
    stat_send, stat_recv, last_send, last_recv,
):
    me = lax.axis_index("blk")
    slots, width = hid.shape
    chunks = width // 128
    piece = slots * chunks
    row_count = n * slots
    block = weight.shape[0] // blocks
    near_size, high_size = layout_of(n)
    near = lax.rem(me, near_size)
    high = me // near_size
    core = lax.rem(near, 2)
    plane = near // 2
    planes = near_size // 2

    loads = [
        pltpu.make_async_copy(source, target, load_sem.at[index])
        for index, (source, target) in enumerate(
            zip(
                (hidden_ref, gain_ref, targets_ref, spans_ref),
                (hid, gain, small_targets, small_spans),
            )
        )
    ]
    for load in loads:
        load.start()

    def weight_copy(index):
        where = pl.ds(index * block, block)
        return pltpu.make_async_copy(weight_ref.at[where], weight.at[where], weight_sem.at[index])

    for index in range(blocks):
        weight_copy(index).start()

    def device(high_index, near_index):
        return (high_index * near_size + near_index,)

    def other_high(step):
        return lax.rem(high + step, high_size)

    def other_near(step):
        return lax.rem(near + step, near_size)

    def other_plane(step):
        return lax.rem(plane + step, planes) * 2

    barrier = pltpu.get_barrier_semaphore()

    @pl.loop(1, high_size)
    def _(step):
        pl.semaphore_signal(
            barrier, inc=1, device_id=device(other_high(step), near), device_id_type=MESH
        )

    for step in range(1, near_size):
        pl.semaphore_signal(
            barrier, inc=1, device_id=device(high, other_near(step)), device_id_type=MESH
        )

    loads[0].wait()
    values = hid[...].astype(jnp.float32)
    meansq = jnp.mean(values * values, axis=-1, keepdims=True)
    values = values * lax.rsqrt(meansq + epsilon)
    mine = wide.at[0]
    for chunk in range(chunks):
        mine[:, chunk, :] = values[:, chunk * 128 : (chunk + 1) * 128]
    loads[1].wait()
    normed = (mine[...] * gain[...][None]).astype(jnp.bfloat16)
    rows[near, high] = normed.reshape(piece, 128)

    loads[2].wait()
    loads[3].wait()
    lanes = lax.broadcasted_iota(jnp.int32, (1, all_targets.shape[-1]), 1)
    spread = jnp.zeros(lanes.shape, jnp.int32)
    for slot in range(slots):
        place = slot * n + near * high_size + high
        spread = jnp.where(lanes == place, small_targets[slot], spread)
    all_targets[near, high] = spread

    pl.semaphore_wait(barrier, high_size + near_size - 2)

    def remote(source, target, send_sem, recv_sem, device_id):
        return pltpu.make_async_remote_copy(
            src_ref=source,
            dst_ref=target,
            send_sem=send_sem,
            recv_sem=recv_sem,
            device_id=device_id,
            device_id_type=MESH,
        )

    def drain(ref, semaphore):
        pltpu.make_async_copy(ref, ref, semaphore).wait()

    @pl.loop(1, high_size)
    def _(step):
        view = rows.at[near, high]
        remote(view, view, row_send, high_recv, device(other_high(step), near)).start()

    @pl.loop(1, high_size)
    def _(step):
        view = all_targets.at[near, high]
        remote(view, view, target_send, target_high, device(other_high(step), near)).start()

    if high_size > 1:
        drain(rows.at[0, pl.ds(0, high_size - 1)], high_recv)
    own = rows.at[near]
    for step in range(1, planes):
        remote(
            own, own, row_send, near_recv.at[planes - step], device(high, other_plane(step) + core)
        ).start()
    remote(own, own, row_send, near_recv.at[0], device(high, plane * 2 + 1 - core)).start()
    if high_size > 1:
        drain(all_targets.at[0, pl.ds(0, high_size - 1)], target_high)
    own = all_targets.at[near]
    for step in range(1, near_size):
        remote(own, own, target_send, target_near, device(high, other_near(step))).start()
    for step in range(1, planes):
        view = rows.at[other_plane(step) + core]
        remote(view, view, row_send, near_recv.at[step], device(high, near)).wait_recv()
        remote(
            view, view, row_send, far_recv.at[step], device(high, plane * 2 + 1 - core)
        ).start()

    near_view = rows.at[plane * 2 + 1 - core]
    remote(near_view, near_view, row_send, near_recv.at[0], device(high, near)).wait_recv()
    for step in range(1, planes):
        view = rows.at[other_plane(step) + 1 - core]
        remote(view, view, row_send, far_recv.at[step], device(high, near)).wait_recv()

    group = wide.shape[0]

    @pl.loop(0, n // group)
    def _(index):
        if group >= high_size:
            count = group // high_size
            block_rows = rows[pl.ds(index * count, count)]
        else:
            count = high_size // group
            block_rows = rows[index // count, pl.ds(lax.rem(index, count) * group, group)]
        wide[...] = block_rows.astype(jnp.float32).reshape(group, slots, chunks, 128)
        for slot in range(slots):
            place = pl.ds(pl.multiple_of(slot * n + index * group, group), group)
            for chunk in range(chunks):
                operand[place, chunk * 128 : (chunk + 1) * 128] = wide[:, slot, chunk, :].astype(
                    jnp.bfloat16
                )

    def multiply(index):
        weight_copy(index).wait()
        where = pl.ds(index * block, block)
        logits[where, :] = lax.dot_general(
            weight[where, :],
            operand[...],
            (((1,), (1,)), ((), ())),
            preferred_element_type=jnp.float32,
        )

    multiply(0)
    drain(all_targets.at[pl.ds(0, near_size - 1)], target_near)
    wanted = all_targets[...].reshape(n, -1)
    wanted = jnp.sum(wanted, axis=0, keepdims=True)[:, :row_count] - me * weight.shape[0]

    def stats(index):
        found = logits[pl.ds(index * block, block), :]
        column = lax.broadcasted_iota(jnp.int32, found.shape, 0)
        peak = jnp.max(found, axis=0, keepdims=True)
        expon = jnp.exp(found - peak)
        return (
            peak,
            jnp.sum(expon, axis=0, keepdims=True),
            jnp.sum(expon * found, axis=0, keepdims=True),
            jnp.sum(
                jnp.where(column == wanted - index * block, found, 0.0), axis=0, keepdims=True
            ),
        )

    parts = []
    for index in range(blocks):
        if index + 1 < blocks:
            multiply(index + 1)
        parts.append(stats(index))
    peak = functools.reduce(jnp.maximum, [part[0] for part in parts])
    scales = [jnp.exp(part[0] - peak) for part in parts]
    total = sum(part[1] * scale for part, scale in zip(parts, scales))
    moment = sum(part[2] * scale for part, scale in zip(parts, scales))
    picked = sum(part[3] for part in parts)

    def by_slot(item):
        return [item[:, slot * n : (slot + 1) * n] for slot in range(slots)]

    blank = [jnp.zeros((1, n), jnp.float32)] * slots
    packed = jnp.concatenate(
        by_slot(total) + by_slot(moment) + by_slot(picked) + blank
        + by_slot(peak) + by_slot(peak) + blank + blank,
        axis=0,
    )
    fields = packed.shape[0]
    turned = jnp.concatenate([packed.T, jnp.zeros((n, 128 - fields), jnp.float32)], axis=1)
    for index in range(near_size):
        message[index] = turned[index * high_size : (index + 1) * high_size]

    inbox[near] = message[near]
    for step in range(1, near_size):
        remote(
            message.at[other_near(step)], inbox.at[near], stat_send, stat_recv,
            device(high, other_near(step)),
        ).start()
    drain(inbox.at[pl.ds(0, near_size - 1)], stat_recv)

    def merge(arrived, axis):
        peaks = pltpu.roll(arrived, 128 - fields // 2, arrived.ndim - 1)
        top = jnp.max(peaks, axis=axis)
        return jnp.sum(arrived * jnp.exp(peaks - top[None]), axis=axis), top

    arrived = inbox[...]
    merged, _ = merge(arrived, 0)
    lane = lax.broadcasted_iota(jnp.int32, merged.shape, 1)
    merged = jnp.where(lane < fields // 2, merged, jnp.max(arrived, axis=0))
    onward[...] = merged.reshape(high_size, 1, 128)
    last[high] = onward[high]

    @pl.loop(1, high_size)
    def _(step):
        remote(
            onward.at[other_high(step)], last.at[high], last_send, last_recv,
            device(other_high(step), near),
        ).start()

    if high_size > 1:
        drain(last.at[pl.ds(0, high_size - 1)], last_recv)
    merged, top = merge(last[...].reshape(high_size, 128), 0)
    merged, top = merged[None], top[None]
    lse = top + jnp.log(merged)
    expected = pltpu.roll(merged, 128 - slots, 1) / merged
    chosen = pltpu.roll(merged, 128 - 2 * slots, 1)
    slot_ids = lax.broadcasted_iota(jnp.int32, (1, 128), 1)
    scored = (slot_ids >= small_spans[0, 0]) & (slot_ids < small_spans[0, 1])
    out_ref[0:1, :] = jnp.where(scored, chosen - lse, 0.0)
    out_ref[1:2, :] = jnp.where(scored, lse - expected, 0.0)

    for step in range(2 * planes - 1):
        drain(rows.at[0], row_send)
    if high_size > 1:
        drain(rows.at[0, pl.ds(0, high_size - 1)], row_send)
        drain(all_targets.at[0, pl.ds(0, high_size - 1)], target_send)
        drain(last.at[pl.ds(0, high_size - 1)], last_send)
    drain(all_targets.at[pl.ds(0, near_size - 1)], target_send)
    drain(inbox.at[pl.ds(0, near_size - 1)], stat_send)


def local(n, hidden, norm_gain, head_weight, targets, spans):
    slots, width = hidden.shape
    vocab = head_weight.shape[0]
    chunks = width // 128
    piece = slots * chunks
    row_count = n * slots
    blocks = vocab // largest_block(vocab, 800, 16)
    lanes = max(128, row_count)
    near_size, high_size = layout_of(n)
    group = min(n, 32)
    out = pl.pallas_call(
        functools.partial(kernel, n, blocks),
        out_shape=jax.ShapeDtypeStruct((2, 128), jnp.float32),
        in_specs=[pl.BlockSpec(memory_space=pltpu.HBM)] * 5,
        out_specs=pl.BlockSpec(memory_space=pltpu.VMEM),
        scratch_shapes=[
            pltpu.VMEM((slots, width), jnp.bfloat16),
            pltpu.VMEM((chunks, 128), jnp.float32),
            pltpu.VMEM((vocab, width), jnp.bfloat16),
            pltpu.SMEM(targets.shape, jnp.int32),
            pltpu.SMEM(spans.shape, jnp.int32),
            pltpu.VMEM((near_size, high_size, piece, 128), jnp.bfloat16),
            pltpu.VMEM((group, slots, chunks, 128), jnp.float32),
            pltpu.VMEM((row_count, width), jnp.bfloat16),
            pltpu.VMEM((vocab, row_count), jnp.float32),
            pltpu.VMEM((near_size, high_size, 1, lanes), jnp.int32),
            pltpu.VMEM((near_size, high_size, 128), jnp.float32),
            pltpu.VMEM((near_size, high_size, 128), jnp.float32),
            pltpu.VMEM((high_size, 1, 128), jnp.float32),
            pltpu.VMEM((high_size, 1, 128), jnp.float32),
            pltpu.SemaphoreType.DMA((4,)),
            pltpu.SemaphoreType.DMA((blocks,)),
            pltpu.SemaphoreType.DMA,
            pltpu.SemaphoreType.DMA,
            pltpu.SemaphoreType.DMA((near_size // 2,)),
            pltpu.SemaphoreType.DMA((near_size // 2,)),
            pltpu.SemaphoreType.DMA,
            pltpu.SemaphoreType.DMA,
            pltpu.SemaphoreType.DMA,
            pltpu.SemaphoreType.DMA,
            pltpu.SemaphoreType.DMA,
            pltpu.SemaphoreType.DMA,
            pltpu.SemaphoreType.DMA,
        ],
        compiler_params=pltpu.CompilerParams(
            collective_id=0, has_side_effects=True, vmem_limit_bytes=60 * 2**20
        ),
        name="head_stats",
    )(hidden, norm_gain.reshape(chunks, 128), head_weight, targets, spans)
    return out[0, :slots], out[1, :slots]


def solution(mesh):
    return jax.shard_map(
        functools.partial(local, mesh.shape["blk"]),
        mesh=mesh,
        in_specs=(P("blk", None), P(), P("blk", None), P("blk"), P("blk", None)),
        out_specs=(P("blk"), P("blk")),
        check_vma=False,
    )
```

time: 33.6 us -> 31.3 us (0.932)
  local copies, waits for them, and re-layouts: 3.72 us -> 1.25 us
    unnamed x10 -> x0, local copies, waits for them, and re-layouts: 3.72 us -> none
    squeeze x0 -> x1, local copies, waits for them, and re-layouts: none -> 1.25 us  [local(): return (out[0, :slots], out[1, :slots])]
where the time goes in v2:
time: 31.3 us; the launch traced here: 31.1 us
  Pallas kernels  29.2 us (93%)
  local copies, waits for them, and re-layouts  1.25 us (4%)
  between operations  0.64 us (2%)
    pallas_call x1, Pallas kernels, local(): pl.pallas_call(functools.partial(kernel, n, blocks), out_shape=jax.ShapeD...  29.2 us
    squeeze x1, local copies, waits for them, and re-layouts, local(): return (out[0, :slots], out[1, :slots])  1.25 us

profile of v2, /device:TPU:0, one launch (start us, length us, event | category | flops | bytes accessed | tf_op | source)
XLA Modules:
  0.0 31.1 jit_solution(4618378302528633424)
XLA Ops:
  0.6 29.2 %head_stats.1 = f32[2,128]{1,0:T(2,128)} custom-call(bf16[2,2048]{1,0:T(2,128)(2,1)} %hidden_ref.1, f32[16,128]{1,0:T(8,128)} %bitcast.5, bf16[3200,2048]{1,0:T(8,128)(2,1)} %weight_ref.1, s32[2]{0:T(128)} %targets_ref.1, s32[1,2]{1,0:T(1,128)} %spans_ref.1), custom_call_target="tpu_custom_call" | custom-call | tf_op jit(solution)/shard_map/head_stats/pallas_call | solution.py:290
  29.8 1.3 %slice_bitcast_fusion = (f32[2]{0:T(128)}, f32[2]{0:T(128)}) fusion(f32[2,128]{1,0:T(2,128)} %head_stats.1), kind=kLoop, calls=%fused_computation | loop fusion | bytes 32 | tf_op jit(solution)/shard_map/squeeze | solution.py:329

commit v3 on v2

--- a/solution.py
+++ b/solution.py
@@ -23,10 +23,10 @@
 
 def kernel(
     n, blocks, hidden_ref, gain_ref, weight_ref, targets_ref, spans_ref, out_ref,
-    hid, gain, weight, small_targets, small_spans, rows, wide, operand, logits,
-    all_targets, message, inbox, onward, last, load_sem, weight_sem,
+    hid, gain, weight, small_targets, small_spans, rows, wide, operand,
+    all_targets, message, inbox, load_sem, weight_sem,
     row_send, high_recv, near_recv, far_recv, target_send, target_high, target_near,
-    stat_send, stat_recv, last_send, last_recv,
+    stat_send, stat_recv,
 ):
     me = lax.axis_index("blk")
     slots, width = hid.shape
@@ -74,16 +74,9 @@
 
     barrier = pltpu.get_barrier_semaphore()
 
-    @pl.loop(1, high_size)
-    def _(step):
-        pl.semaphore_signal(
-            barrier, inc=1, device_id=device(other_high(step), near), device_id_type=MESH
-        )
-
-    for step in range(1, near_size):
-        pl.semaphore_signal(
-            barrier, inc=1, device_id=device(high, other_near(step)), device_id_type=MESH
-        )
+    @pl.loop(1, n)
+    def _(step):
+        pl.semaphore_signal(barrier, inc=1, device_id=(lax.rem(me + step, n),), device_id_type=MESH)
 
     loads[0].wait()
     values = hid[...].astype(jnp.float32)
@@ -105,7 +98,7 @@
         spread = jnp.where(lanes == place, small_targets[slot], spread)
     all_targets[near, high] = spread
 
-    pl.semaphore_wait(barrier, high_size + near_size - 2)
+    pl.semaphore_wait(barrier, n - 1)
 
     def remote(source, target, send_sem, recv_sem, device_id):
         return pltpu.make_async_remote_copy(
@@ -174,45 +167,35 @@
                     jnp.bfloat16
                 )
 
-    def multiply(index):
+    drain(all_targets.at[pl.ds(0, near_size - 1)], target_near)
+    wanted = all_targets[...].reshape(n, -1)
+    wanted = jnp.sum(wanted, axis=0, keepdims=True)[:, :row_count] - me * weight.shape[0]
+
+    def step_block(index, carry):
         weight_copy(index).wait()
-        where = pl.ds(index * block, block)
-        logits[where, :] = lax.dot_general(
+        where = pl.ds(pl.multiple_of(index * block, block), block)
+        found = lax.dot_general(
             weight[where, :],
             operand[...],
             (((1,), (1,)), ((), ())),
             preferred_element_type=jnp.float32,
         )
-
-    multiply(0)
-    drain(all_targets.at[pl.ds(0, near_size - 1)], target_near)
-    wanted = all_targets[...].reshape(n, -1)
-    wanted = jnp.sum(wanted, axis=0, keepdims=True)[:, :row_count] - me * weight.shape[0]
-
-    def stats(index):
-        found = logits[pl.ds(index * block, block), :]
         column = lax.broadcasted_iota(jnp.int32, found.shape, 0)
-        peak = jnp.max(found, axis=0, keepdims=True)
+        peak = jnp.maximum(carry[0], jnp.max(found, axis=0, keepdims=True))
+        scale = jnp.exp(carry[0] - peak)
         expon = jnp.exp(found - peak)
+        chosen = jnp.where(column == wanted - index * block, found, 0.0)
         return (
             peak,
-            jnp.sum(expon, axis=0, keepdims=True),
-            jnp.sum(expon * found, axis=0, keepdims=True),
-            jnp.sum(
-                jnp.where(column == wanted - index * block, found, 0.0), axis=0, keepdims=True
-            ),
-        )
-
-    parts = []
-    for index in range(blocks):
-        if index + 1 < blocks:
-            multiply(index + 1)
-        parts.append(stats(index))
-    peak = functools.reduce(jnp.maximum, [part[0] for part in parts])
-    scales = [jnp.exp(part[0] - peak) for part in parts]
-    total = sum(part[1] * scale for part, scale in zip(parts, scales))
-    moment = sum(part[2] * scale for part, scale in zip(parts, scales))
-    picked = sum(part[3] for part in parts)
+            carry[1] * scale + jnp.sum(expon, axis=0, keepdims=True),
+            carry[2] * scale + jnp.sum(expon * found, axis=0, keepdims=True),
+            carry[3] + jnp.sum(chosen, axis=0, keepdims=True),
+        )
+
+    zero = jnp.zeros((1, row_count), jnp.float32)
+    peak, total, moment, picked = lax.fori_loop(
+        0, blocks, step_block, (jnp.full((1, row_count), -jnp.inf, jnp.float32), zero, zero, zero)
+    )
 
     def by_slot(item):
         return [item[:, slot * n : (slot + 1) * n] for slot in range(slots)]
@@ -225,40 +208,23 @@
     )
     fields = packed.shape[0]
     turned = jnp.concatenate([packed.T, jnp.zeros((n, 128 - fields), jnp.float32)], axis=1)
-    for index in range(near_size):
-        message[index] = turned[index * high_size : (index + 1) * high_size]
-
-    inbox[near] = message[near]
-    for step in range(1, near_size):
+    message[...] = turned.reshape(n, 1, 128)
+    mine_at = near * high_size + high
+    inbox[mine_at] = message[mine_at]
+
+    @pl.loop(1, n)
+    def _(step):
+        other = lax.rem(me + step, n)
         remote(
-            message.at[other_near(step)], inbox.at[near], stat_send, stat_recv,
-            device(high, other_near(step)),
+            message.at[lax.rem(other, near_size) * high_size + other // near_size],
+            inbox.at[mine_at], stat_send, stat_recv, (other,),
         ).start()
-    drain(inbox.at[pl.ds(0, near_size - 1)], stat_recv)
-
-    def merge(arrived, axis):
-        peaks = pltpu.roll(arrived, 128 - fields // 2, arrived.ndim - 1)
-        top = jnp.max(peaks, axis=axis)
-        return jnp.sum(arrived * jnp.exp(peaks - top[None]), axis=axis), top
-
-    arrived = inbox[...]
-    merged, _ = merge(arrived, 0)
-    lane = lax.broadcasted_iota(jnp.int32, merged.shape, 1)
-    merged = jnp.where(lane < fields // 2, merged, jnp.max(arrived, axis=0))
-    onward[...] = merged.reshape(high_size, 1, 128)
-    last[high] = onward[high]
-
-    @pl.loop(1, high_size)
-    def _(step):
-        remote(
-            onward.at[other_high(step)], last.at[high], last_send, last_recv,
-            device(other_high(step), near),
-        ).start()
-
-    if high_size > 1:
-        drain(last.at[pl.ds(0, high_size - 1)], last_recv)
-    merged, top = merge(last[...].reshape(high_size, 128), 0)
-    merged, top = merged[None], top[None]
+
+    drain(inbox.at[pl.ds(0, n - 1)], stat_recv)
+    arrived = inbox[...].reshape(n, 128)
+    peaks = pltpu.roll(arrived, 128 - fields // 2, 1)
+    top = jnp.max(peaks, axis=0, keepdims=True)
+    merged = jnp.sum(arrived * jnp.exp(peaks - top), axis=0, keepdims=True)
     lse = top + jnp.log(merged)
     expected = pltpu.roll(merged, 128 - slots, 1) / merged
     chosen = pltpu.roll(merged, 128 - 2 * slots, 1)
@@ -272,9 +238,8 @@
     if high_size > 1:
         drain(rows.at[0, pl.ds(0, high_size - 1)], row_send)
         drain(all_targets.at[0, pl.ds(0, high_size - 1)], target_send)
-        drain(last.at[pl.ds(0, high_size - 1)], last_send)
     drain(all_targets.at[pl.ds(0, near_size - 1)], target_send)
-    drain(inbox.at[pl.ds(0, near_size - 1)], stat_send)
+    drain(inbox.at[pl.ds(0, n - 1)], stat_send)
 
 
 def local(n, hidden, norm_gain, head_weight, targets, spans):
@@ -283,7 +248,7 @@
     chunks = width // 128
     piece = slots * chunks
     row_count = n * slots
-    blocks = vocab // largest_block(vocab, 800, 16)
+    blocks = vocab // largest_block(vocab, 640, 16)
     lanes = max(128, row_count)
     near_size, high_size = layout_of(n)
     group = min(n, 32)
@@ -301,20 +266,15 @@
             pltpu.VMEM((near_size, high_size, piece, 128), jnp.bfloat16),
             pltpu.VMEM((group, slots, chunks, 128), jnp.float32),
             pltpu.VMEM((row_count, width), jnp.bfloat16),
-            pltpu.VMEM((vocab, row_count), jnp.float32),
             pltpu.VMEM((near_size, high_size, 1, lanes), jnp.int32),
-            pltpu.VMEM((near_size, high_size, 128), jnp.float32),
-            pltpu.VMEM((near_size, high_size, 128), jnp.float32),
-            pltpu.VMEM((high_size, 1, 128), jnp.float32),
-            pltpu.VMEM((high_size, 1, 128), jnp.float32),
+            pltpu.VMEM((n, 1, 128), jnp.float32),
+            pltpu.VMEM((n, 1, 128), jnp.float32),
             pltpu.SemaphoreType.DMA((4,)),
             pltpu.SemaphoreType.DMA((blocks,)),
             pltpu.SemaphoreType.DMA,
             pltpu.SemaphoreType.DMA,
             pltpu.SemaphoreType.DMA((near_size // 2,)),
             pltpu.SemaphoreType.DMA((near_size // 2,)),
-            pltpu.SemaphoreType.DMA,
-            pltpu.SemaphoreType.DMA,
             pltpu.SemaphoreType.DMA,
             pltpu.SemaphoreType.DMA,
             pltpu.SemaphoreType.DMA,

time: 31.3 us -> 27.9 us (0.89)
  Pallas kernels: 29.2 us -> 25.9 us
    pallas_call x1, Pallas kernels: 29.2 us -> 25.9 us  [local(): pl.pallas_call(functools.partial(kernel, n, blocks), out_shape=jax.ShapeD...]
where the time goes in v3:
time: 27.9 us; the launch traced here: 27.8 us
  Pallas kernels  25.9 us (93%)
  local copies, waits for them, and re-layouts  1.25 us (4%)
  between operations  0.64 us (2%)
    pallas_call x1, Pallas kernels, local(): pl.pallas_call(functools.partial(kernel, n, blocks), out_shape=jax.ShapeD...  25.9 us
    squeeze x1, local copies, waits for them, and re-layouts, local(): return (out[0, :slots], out[1, :slots])  1.25 us

profile of v3, /device:TPU:0, one launch (start us, length us, event | category | flops | bytes accessed | tf_op | source)
XLA Modules:
  0.0 27.8 jit_solution(3085425770166985329)
XLA Ops:
  0.6 25.9 %head_stats.1 = f32[2,128]{1,0:T(2,128)} custom-call(bf16[2,2048]{1,0:T(2,128)(2,1)} %hidden_ref.1, f32[16,128]{1,0:T(8,128)} %bitcast.5, bf16[3200,2048]{1,0:T(8,128)(2,1)} %weight_ref.1, s32[2]{0:T(128)} %targets_ref.1, s32[1,2]{1,0:T(1,128)} %spans_ref.1), custom_call_target="tpu_custom_call" | custom-call | tf_op jit(solution)/shard_map/head_stats/pallas_call | solution.py:255
  26.5 1.3 %slice_bitcast_fusion = (f32[2]{0:T(128)}, f32[2]{0:T(128)}) fusion(f32[2,128]{1,0:T(2,128)} %head_stats.1), kind=kLoop, calls=%fused_computation | loop fusion | bytes 32 | tf_op jit(solution)/shard_map/squeeze | solution.py:289

commit v4 on v3

--- a/solution.py
+++ b/solution.py
@@ -74,9 +74,20 @@
 
     barrier = pltpu.get_barrier_semaphore()
 
-    @pl.loop(1, n)
-    def _(step):
-        pl.semaphore_signal(barrier, inc=1, device_id=(lax.rem(me + step, n),), device_id_type=MESH)
+    nears = [other_near(step) for step in range(near_size)]
+
+    def greet(high_index, near_index):
+        pl.semaphore_signal(
+            barrier, inc=1, device_id=device(high_index, near_index), device_id_type=MESH
+        )
+
+    for near_index in nears[1:]:
+        greet(high, near_index)
+
+    @pl.loop(1, high_size)
+    def _(step):
+        for near_index in nears:
+            greet(other_high(step), near_index)
 
     loads[0].wait()
     values = hid[...].astype(jnp.float32)
@@ -113,41 +124,44 @@
     def drain(ref, semaphore):
         pltpu.make_async_copy(ref, ref, semaphore).wait()
 
+    def send_row(high_index, turn):
+        view = rows.at[near, high]
+        remote(
+            view, view, row_send, near_recv.at[(planes - turn) % planes],
+            device(high_index, other_plane(turn) + core),
+        ).start()
+
     @pl.loop(1, high_size)
     def _(step):
-        view = rows.at[near, high]
-        remote(view, view, row_send, high_recv, device(other_high(step), near)).start()
+        for turn in range(planes):
+            send_row(other_high(step), turn)
+
+    for turn in range(1, planes):
+        send_row(high, turn)
 
     @pl.loop(1, high_size)
     def _(step):
         view = all_targets.at[near, high]
         remote(view, view, target_send, target_high, device(other_high(step), near)).start()
 
-    if high_size > 1:
-        drain(rows.at[0, pl.ds(0, high_size - 1)], high_recv)
-    own = rows.at[near]
-    for step in range(1, planes):
-        remote(
-            own, own, row_send, near_recv.at[planes - step], device(high, other_plane(step) + core)
-        ).start()
-    remote(own, own, row_send, near_recv.at[0], device(high, plane * 2 + 1 - core)).start()
     if high_size > 1:
         drain(all_targets.at[0, pl.ds(0, high_size - 1)], target_high)
     own = all_targets.at[near]
-    for step in range(1, near_size):
+
+    @pl.loop(1, near_size)
+    def _(step):
         remote(own, own, target_send, target_near, device(high, other_near(step))).start()
-    for step in range(1, planes):
+
+    mate = device(high, plane * 2 + 1 - core)
+    if high_size > 1:
+        drain(rows.at[0, pl.ds(0, high_size - 1)], near_recv.at[0])
+    for step in range(planes):
         view = rows.at[other_plane(step) + core]
-        remote(view, view, row_send, near_recv.at[step], device(high, near)).wait_recv()
-        remote(
-            view, view, row_send, far_recv.at[step], device(high, plane * 2 + 1 - core)
-        ).start()
-
-    near_view = rows.at[plane * 2 + 1 - core]
-    remote(near_view, near_view, row_send, near_recv.at[0], device(high, near)).wait_recv()
-    for step in range(1, planes):
-        view = rows.at[other_plane(step) + 1 - core]
-        remote(view, view, row_send, far_recv.at[step], device(high, near)).wait_recv()
+        if step > 0:
+            drain(view, near_recv.at[step])
+        remote(view, view, row_send, far_recv.at[step], mate).start()
+    for step in range(planes):
+        drain(rows.at[other_plane(step) + 1 - core], far_recv.at[step])
 
     group = wide.shape[0]
 
@@ -212,13 +226,19 @@
     mine_at = near * high_size + high
     inbox[mine_at] = message[mine_at]
 
-    @pl.loop(1, n)
-    def _(step):
-        other = lax.rem(me + step, n)
+    def send_stats(high_index, near_index):
         remote(
-            message.at[lax.rem(other, near_size) * high_size + other // near_size],
-            inbox.at[mine_at], stat_send, stat_recv, (other,),
+            message.at[near_index * high_size + high_index], inbox.at[mine_at],
+            stat_send, stat_recv, device(high_index, near_index),
         ).start()
+
+    @pl.loop(1, high_size)
+    def _(step):
+        for near_index in nears:
+            send_stats(other_high(step), near_index)
+
+    for near_index in nears[1:]:
+        send_stats(high, near_index)
 
     drain(inbox.at[pl.ds(0, n - 1)], stat_recv)
     arrived = inbox[...].reshape(n, 128)
@@ -248,7 +268,7 @@
     chunks = width // 128
     piece = slots * chunks
     row_count = n * slots
-    blocks = vocab // largest_block(vocab, 640, 16)
+    blocks = vocab // largest_block(vocab, 1600, 16)
     lanes = max(128, row_count)
     near_size, high_size = layout_of(n)
     group = min(n, 32)

time: 27.9 us -> 27.1 us (0.971)
  Pallas kernels: 25.9 us -> 24.9 us
    pallas_call x1, Pallas kernels: 25.9 us -> 24.9 us  [local(): pl.pallas_call(functools.partial(kernel, n, blocks), out_shape=jax.ShapeD...]
where the time goes in v4:
time: 27.1 us; the launch traced here: 26.8 us
  Pallas kernels  24.9 us (92%)
  local copies, waits for them, and re-layouts  1.25 us (5%)
  between operations  0.64 us (2%)
    pallas_call x1, Pallas kernels, local(): pl.pallas_call(functools.partial(kernel, n, blocks), out_shape=jax.ShapeD...  24.9 us
    squeeze x1, local copies, waits for them, and re-layouts, local(): return (out[0, :slots], out[1, :slots])  1.25 us

profile of v4, /device:TPU:0, one launch (start us, length us, event | category | flops | bytes accessed | tf_op | source)
XLA Modules:
  0.0 26.8 jit_solution(11780195920617767094)
XLA Ops:
  0.6 24.9 %head_stats.1 = f32[2,128]{1,0:T(2,128)} custom-call(bf16[2,2048]{1,0:T(2,128)(2,1)} %hidden_ref.1, f32[16,128]{1,0:T(8,128)} %bitcast.5, bf16[3200,2048]{1,0:T(8,128)(2,1)} %weight_ref.1, s32[2]{0:T(128)} %targets_ref.1, s32[1,2]{1,0:T(1,128)} %spans_ref.1), custom_call_target="tpu_custom_call" | custom-call | tf_op jit(solution)/shard_map/head_stats/pallas_call | solution.py:275
  25.6 1.3 %slice_bitcast_fusion = (f32[2]{0:T(128)}, f32[2]{0:T(128)}) fusion(f32[2,128]{1,0:T(2,128)} %head_stats.1), kind=kLoop, calls=%fused_computation | loop fusion | bytes 32 | tf_op jit(solution)/shard_map/squeeze | solution.py:309

commit v5 on v4

--- a/solution.py
+++ b/solution.py
@@ -22,7 +22,7 @@
 
 
 def kernel(
-    n, blocks, hidden_ref, gain_ref, weight_ref, targets_ref, spans_ref, out_ref,
+    n, blocks, hidden_ref, gain_ref, weight_ref, targets_ref, spans_ref, logprob_ref, entropy_ref,
     hid, gain, weight, small_targets, small_spans, rows, wide, operand,
     all_targets, message, inbox, load_sem, weight_sem,
     row_send, high_recv, near_recv, far_recv, target_send, target_high, target_near,
@@ -250,8 +250,8 @@
     chosen = pltpu.roll(merged, 128 - 2 * slots, 1)
     slot_ids = lax.broadcasted_iota(jnp.int32, (1, 128), 1)
     scored = (slot_ids >= small_spans[0, 0]) & (slot_ids < small_spans[0, 1])
-    out_ref[0:1, :] = jnp.where(scored, chosen - lse, 0.0)
-    out_ref[1:2, :] = jnp.where(scored, lse - expected, 0.0)
+    logprob_ref[...] = jnp.where(scored, chosen - lse, 0.0)[:, :slots]
+    entropy_ref[...] = jnp.where(scored, lse - expected, 0.0)[:, :slots]
 
     for step in range(2 * planes - 1):
         drain(rows.at[0], row_send)
@@ -272,11 +272,12 @@
     lanes = max(128, row_count)
     near_size, high_size = layout_of(n)
     group = min(n, 32)
-    out = pl.pallas_call(
+    small = jax.ShapeDtypeStruct((1, slots), jnp.float32)
+    logprob, entropy = pl.pallas_call(
         functools.partial(kernel, n, blocks),
-        out_shape=jax.ShapeDtypeStruct((2, 128), jnp.float32),
+        out_shape=(small, small),
         in_specs=[pl.BlockSpec(memory_space=pltpu.HBM)] * 5,
-        out_specs=pl.BlockSpec(memory_space=pltpu.VMEM),
+        out_specs=(pl.BlockSpec(memory_space=pltpu.VMEM),) * 2,
         scratch_shapes=[
             pltpu.VMEM((slots, width), jnp.bfloat16),
             pltpu.VMEM((chunks, 128), jnp.float32),
@@ -306,7 +307,7 @@
         ),
         name="head_stats",
     )(hidden, norm_gain.reshape(chunks, 128), head_weight, targets, spans)
-    return out[0, :slots], out[1, :slots]
+    return logprob.reshape(slots), entropy.reshape(slots)
 
 
 def solution(mesh):

time: 27.1 us -> 28 us (1.033)
  local copies, waits for them, and re-layouts: 1.25 us -> 2.25 us
    unnamed x0 -> x2, local copies, waits for them, and re-layouts: none -> 2.25 us
    squeeze x1 -> x0, local copies, waits for them, and re-layouts: 1.25 us -> none  [local(): return (out[0, :slots], out[1, :slots])]
where the time goes in v5:
time: 28 us; the launch traced here: 27.8 us
  Pallas kernels  24.9 us (89%)
  local copies, waits for them, and re-layouts  2.25 us (8%)
  between operations  0.64 us (2%)
    pallas_call x1, Pallas kernels, local(): pl.pallas_call(functools.partial(kernel, n, blocks), out_shape=(small, sm...  24.9 us
    unnamed x2, local copies, waits for them, and re-layouts  2.25 us

profile of v5, /device:TPU:0, one launch (start us, length us, event | category | flops | bytes accessed | tf_op | source)
XLA Modules:
  0.0 27.8 jit_solution(12185710827510594896)
XLA Ops:
  0.6 24.9 %head_stats.1 = (f32[1,2]{1,0:T(1,128)}, f32[1,2]{1,0:T(1,128)}) custom-call(bf16[2,2048]{1,0:T(2,128)(2,1)} %hidden_ref.1, f32[16,128]{1,0:T(8,128)} %bitcast.3, bf16[3200,2048]{1,0:T(8,128)(2,1)} %weight_ref.1, s32[2]{0:T(128)} %targets_ref.1, s32[1,2]{1,0:T(1,128)} %spans_ref.1), custom_call_target="tpu_custom_call" | custom-call | tf_op jit(solution)/shard_map/head_stats/pallas_call | solution.py:276
  25.6 1.1 %copy.9 = f32[2]{0:T(128)} copy(f32[2]{0:T(128)} %bitcast.5) | data formatting | bytes 16
  26.7 1.1 %copy.10 = f32[2]{0:T(128)} copy(f32[2]{0:T(128)} %bitcast.4) | data formatting | bytes 16
